TPU v7x, 32 devices: a whole 2x2x4 slice. The times are simulated.
32 devices in a mesh: tok: 16 (over z, x, core), head: 2 (over y).
Axes of the slice: x: 2, y: 2, z: 4, core: 2. Of those that a mesh axis runs over, the one named last changes fastest.
Arguments:
- tokens: bfloat16 [2048, 2560], P('tok', 'head'), may hold values from -6 to 6
- query_weight: bfloat16 [2560, 2560], P('tok'), may hold values from -0.125 to 0.125
- keyvalue_weight: bfloat16 [2560, 512], P('tok'), may hold values from -0.125 to 0.125
- output_weight: bfloat16 [2560, 2560], P(None, ('head', 'tok')), may hold values from -0.125 to 0.125
- cache: bfloat16 [128, 2, 128, 256], P(('tok', 'head')), may hold values from -460 to 460
- page_table: int32 [32, 4], P('tok'), may hold values from 0 to 127, as said below
- parents: int32 [32, 64], P('tok'), may hold values from 0 to 62, as said below
- cache_len: int32 [32], P('tok'), may hold values from 1 to 448, as said below
- accepted_leaf: int32 [32], P('tok'), may hold values from 0 to 63
Outputs:
- attended: bfloat16 [2048, 2560], P('tok', 'head')
- cache_out: bfloat16 [128, 2, 128, 256], P(('tok', 'head'))
Inputs may be any that keep to these rules, and one draw needn't show every extreme that they name: `page_table`: for every d, row d names each of the pages d * 4 to d * 4 + 3 exactly once, so request d's pages all lie on device d (devices counted tok-major, head-minor). parents[r, 0] = 0, and parents[r, i] < i for i >= 1. `cache_len`: roughly half of the requests hold at most 128 cached positions, the others more than 320.
All inputs are finite; a program needn't handle non-finite values.
Results may differ from a plain program's by a relative error of at most 0.014.
The roundings to bfloat16 on the way count: a program that leaves them out, or rounds other values in their place, can miss the bound.
Values may be sent and summed in bfloat16 or wider, within the bound.
A program may use at most 64 MiB of HBM per device.

v0:
```python
import math

import jax
import jax.numpy as jnp
from jax import lax
from jax.sharding import PartitionSpec as P

HQ = 10
HD = 256
DRAFT = 64
PAGE = 128
NPR = 4
WINDOW = 256


def ancestry(parent_row):
    node_ids = jnp.arange(DRAFT, dtype=jnp.int32)
    link = (parent_row[:, None] == node_ids[None, :]).astype(jnp.float32)
    reach = jnp.minimum(link + jnp.eye(DRAFT, dtype=jnp.float32), 1.0)
    for sweep in range((DRAFT - 1).bit_length()):
        reach = jnp.minimum(jnp.dot(reach, reach, precision=lax.Precision.HIGHEST), 1.0)
    depth = (jnp.sum(reach, axis=1) - 1.0).astype(jnp.int32)
    return (reach, depth)


def rotate(values, position):
    half = HD // 4
    freq = jnp.exp(jnp.arange(half, dtype=jnp.float32) * (-2.0 * math.log(10000.0) / (HD // 2)))
    angle = position.astype(jnp.float32)[..., None] * freq
    cosine = jnp.cos(angle)
    sine = jnp.sin(angle)
    first = values[..., :half]
    second = values[..., half : 2 * half]
    return jnp.concatenate(
        [first * cosine - second * sine, second * cosine + first * sine, values[..., 2 * half :]],
        axis=-1,
    )


def attend(queries, cache_keys, cache_values, tree_keys, tree_values, lengths, position, reach):
    window_span = cache_keys.shape[1]
    slot_ids = jnp.arange(window_span, dtype=jnp.int32)
    visible = (slot_ids[None, None, :] < lengths[:, None, None]) & (
        slot_ids[None, None, :] > position[:, :, None] - WINDOW
    )
    cache_scores = jnp.einsum(
        "rnhd,rcd->rhnc", queries, cache_keys, preferred_element_type=jnp.float32
    )
    tree_scores = jnp.einsum(
        "rnhd,rmd->rhnm", queries, tree_keys, preferred_element_type=jnp.float32
    )
    cache_scores = jnp.where(visible[:, None], cache_scores, -1e30)
    tree_scores = jnp.where(reach[:, None] > 0.5, tree_scores, -1e30)
    row_peak = jnp.maximum(jnp.max(cache_scores, axis=-1), jnp.max(tree_scores, axis=-1))[..., None]
    cache_weights = jnp.exp(cache_scores - row_peak)
    tree_weights = jnp.exp(tree_scores - row_peak)
    denominator = jnp.sum(cache_weights, axis=-1, keepdims=True) + jnp.sum(
        tree_weights, axis=-1, keepdims=True
    )
    cache_weights = (cache_weights / denominator).astype(jnp.bfloat16)
    tree_weights = (tree_weights / denominator).astype(jnp.bfloat16)
    result = jnp.einsum(
        "rhnc,rcd->rnhd", cache_weights, cache_values, preferred_element_type=jnp.float32
    )
    result = result + jnp.einsum(
        "rhnm,rmd->rnhd", tree_weights, tree_values, preferred_element_type=jnp.float32
    )
    return result.astype(jnp.bfloat16)


def refresh(logical_pages, length, leaf, reach, depth, new_keys, new_values):
    count = logical_pages.shape[0] * logical_pages.shape[2]
    logical = jnp.transpose(logical_pages, (1, 0, 2, 3)).reshape(2, count, HD)
    slot_ids = jnp.arange(count, dtype=jnp.int32)
    on_path = reach[leaf]
    selector = ((on_path[None, :] > 0.5) & (depth[None, :] == slot_ids[:, None] - length)).astype(
        jnp.float32
    )
    placed_keys = jnp.dot(selector, new_keys.astype(jnp.float32), precision=lax.Precision.HIGHEST)
    placed_values = jnp.dot(
        selector, new_values.astype(jnp.float32), precision=lax.Precision.HIGHEST
    )
    placed = jnp.stack([placed_keys, placed_values]).astype(jnp.bfloat16)
    written = jnp.sum(selector, axis=1) > 0.5
    logical = jnp.where(written[None, :, None], placed, logical)
    return jnp.transpose(
        logical.reshape(2, logical_pages.shape[0], logical_pages.shape[2], HD), (1, 0, 2, 3)
    )


def contract(source, piece):
    return jnp.dot(source, piece, preferred_element_type=jnp.float32)


def project_memory(rows, keyvalue_weight, position):
    projected = contract(rows, lax.all_gather(keyvalue_weight, "tok", axis=0, tiled=True))
    new_keys = rotate(projected[:, :HD], position).astype(jnp.bfloat16)
    new_values = projected[:, HD:].astype(jnp.bfloat16)
    return (new_keys, new_values)


def split_pages(page_blocks, count):
    cache_keys = page_blocks[:, :, 0].reshape(count, NPR * PAGE, HD)
    cache_values = page_blocks[:, :, 1].reshape(count, NPR * PAGE, HD)
    return (cache_keys, cache_values)


def reduce_heads(mixed, output_weight, safe_heads, head_mask, slots_per):
    head_count = lax.axis_size("head")
    tok_count = lax.axis_size("tok")
    narrow = output_weight.shape[1]
    blocks = lax.all_gather(output_weight, "head", axis=1, tiled=True)
    part_cols = blocks.shape[1]
    my_output_weight = (
        jnp.take(blocks.reshape(HQ, HD, part_cols), safe_heads, axis=0) * head_mask[:, None, None]
    )
    my_output_weight = my_output_weight.reshape(slots_per * HD, part_cols)
    partial_value = jnp.dot(
        mixed,
        lax.all_gather(my_output_weight, "tok", axis=1, tiled=True),
        preferred_element_type=jnp.float32,
    ).astype(jnp.bfloat16)
    row_count = partial_value.shape[0]
    partial_value = partial_value.reshape(row_count, tok_count, head_count, narrow)
    partial_value = jnp.transpose(partial_value, (0, 2, 1, 3)).reshape(
        row_count, tok_count * head_count * narrow
    )
    partial_value = lax.optimization_barrier(partial_value)
    summed = lax.psum_scatter(
        partial_value.astype(jnp.float32).astype(jnp.bfloat16),
        "head",
        scatter_dimension=1,
        tiled=True,
    )
    return summed


def shards(
    tokens,
    query_weight,
    keyvalue_weight,
    output_weight,
    cache,
    page_table,
    parents,
    cache_len,
    accepted_leaf,
):
    head_count = lax.axis_size("head")
    head_index = lax.axis_index("head")
    tok_index = lax.axis_index("tok")
    slots_per = -(-HQ // head_count)
    requests = parents.shape[0]
    owned = requests // head_count
    rows_owned = owned * DRAFT
    pages_dev = cache.shape[0]
    gathered = lax.all_gather(tokens, "head", axis=1, tiled=True)
    wide = gathered.astype(jnp.float32)
    mean_square = jnp.mean(wide * wide, axis=1, keepdims=True)
    normed = (wide * lax.rsqrt(mean_square + 1e-06)).astype(jnp.bfloat16)
    reach, depth = jax.vmap(ancestry)(parents)
    position = cache_len[:, None] + depth
    flat_pos = position.reshape(-1)
    head_ids = head_index + head_count * jnp.arange(slots_per, dtype=jnp.int32)
    usable = head_ids < HQ
    safe_heads = jnp.minimum(head_ids, HQ - 1)
    head_mask = usable.astype(jnp.bfloat16)
    part_rows = query_weight.shape[0]
    my_query_weight = (
        jnp.take(query_weight.reshape(part_rows, HQ, HD), safe_heads, axis=1)
        * head_mask[None, :, None]
    )
    my_query_weight = my_query_weight.reshape(part_rows, slots_per * HD)
    queries = contract(normed, lax.all_gather(my_query_weight, "tok", axis=0, tiled=True))
    queries = (rotate(queries.reshape(-1, slots_per, HD), flat_pos[:, None]) * HD ** (-0.5)).astype(
        jnp.bfloat16
    )
    own_start = head_index * rows_owned
    own_reach = lax.dynamic_slice_in_dim(reach, head_index * owned, owned, 0)
    own_depth = lax.dynamic_slice_in_dim(depth, head_index * owned, owned, 0)
    own_len = lax.dynamic_slice_in_dim(cache_len, head_index * owned, owned, 0)
    own_leaf = lax.dynamic_slice_in_dim(accepted_leaf, head_index * owned, owned, 0)
    device = tok_index * head_count + head_index
    own_table = (
        lax.dynamic_slice_in_dim(page_table, head_index * owned, owned, 0) - device * pages_dev
    )
    own_pages = jnp.take(cache, own_table.reshape(-1), axis=0).reshape(owned, NPR, 2, PAGE, HD)
    tree_keys, tree_values = project_memory(normed, keyvalue_weight, flat_pos)
    own_keys = lax.dynamic_slice_in_dim(tree_keys, own_start, rows_owned, 0)
    own_values = lax.dynamic_slice_in_dim(tree_values, own_start, rows_owned, 0)
    page_pool = lax.all_gather(cache, "head", axis=0, tiled=True)
    local_ids = page_table - tok_index * head_count * pages_dev
    page_blocks = jnp.take(page_pool, local_ids.reshape(-1), axis=0).reshape(
        requests, NPR, 2, PAGE, HD
    )
    cache_keys, cache_values = split_pages(page_blocks, requests)
    result = attend(
        queries.reshape(requests, DRAFT, slots_per, HD),
        cache_keys,
        cache_values,
        tree_keys.reshape(requests, DRAFT, HD),
        tree_values.reshape(requests, DRAFT, HD),
        cache_len,
        position,
        reach,
    )
    mixed = result.reshape(-1, slots_per * HD)
    attended = reduce_heads(mixed, output_weight, safe_heads, head_mask, slots_per)
    new_pages = jax.vmap(refresh)(
        own_pages,
        own_len,
        own_leaf,
        own_reach,
        own_depth,
        own_keys.reshape(owned, DRAFT, HD),
        own_values.reshape(owned, DRAFT, HD),
    )
    flat_ids = own_table.reshape(-1)
    matches = (flat_ids[:, None] == jnp.arange(pages_dev, dtype=jnp.int32)[None, :]).astype(
        jnp.int32
    )
    inverse = jnp.sum(matches * jnp.arange(pages_dev, dtype=jnp.int32)[:, None], axis=0)
    cache_out = jnp.take(new_pages.reshape(pages_dev, 2, PAGE, HD), inverse, axis=0)
    return (attended, cache_out)


def solution(mesh):
    in_specs = (
        P("tok", "head"),
        P("tok", None),
        P("tok", None),
        P(None, ("head", "tok")),
        P(("tok", "head"), None, None, None),
        P("tok", None),
        P("tok", None),
        P("tok"),
        P("tok"),
    )
    out_specs = (P("tok", "head"), P(("tok", "head"), None, None, None))
    return jax.shard_map(shards, mesh=mesh, in_specs=in_specs, out_specs=out_specs, check_vma=False)
```

profile of v0, /device:TPU:0, one launch (start us, length us, event | category | flops | bytes accessed | tf_op | source)
XLA Modules:
  0.0 241.8 jit_solution(8897220113036979946)
XLA Ops:
  7.2 0.7 all-gather.5.cloned.1.call-update
  7.9 0.7 all-gather.9.cloned.1.call-update
  8.9 1.2 copy.94
  10.1 0.6 gather_fusion.1
  10.8 0.8 select_multiply_fusion.1
  11.8 17.6 %all_gather.22 = bf16[2560,160]{0,1:T(8,128)(2,1)S(1)} all-gather(bf16[2560,80]{0,1:T(8,128)(2,1)S(1)} %copy-done.1), channel_id=1, replica_groups=mesh['tok'=16,'head'=2] {'head'}, dimensions={1}, use_global_device_ids=true | all-gather | bytes 1228800 | tf_op jit(solution)/shard_map/all_gather | solution.py:112
  29.4 0.6 gather_fusion.2
  30.1 0.8 select_multiply_fusion
  30.9 0.7 dynamic_slice.22
  33.0 0.6 dynamic_slice.24
  35.3 0.6 gather_fusion.3
  37.0 0.7 iota_subtract_fusion
  37.8 8.2 %all_gather.19 = bf16[128,2560]{1,0:T(8,128)(2,1)S(1)} all-gather(bf16[128,1280]{1,0:T(8,128)(2,1)S(1)} %copy-done.2), channel_id=1, replica_groups=mesh['tok'=16,'head'=2] {'head'}, dimensions={1}, use_global_device_ids=true | all-gather | bytes 983040 | tf_op jit(solution)/shard_map/all_gather | solution.py:157
  46.5 1.9 gather_fusion
  48.6 34.7 %all-gather.9.cloned.1.call-done = bf16[2560,512]{1,0:T(8,128)(2,1)} async-done(((bf16[160,512]{1,0:T(8,128)(2,1)}), bf16[2560,512]{1,0:T(8,128)(2,1)}) %all-gather.9.cloned.1.call-update) | async-done | bytes 2621456 | tf_op jit(solution)/shard_map/all_gather | solution.py:96
  83.3 2.3 fusion.12
  85.7 0.3 subtract_convert_fusion
  86.1 62.2 %all-gather.7.cloned.1.call-done = bf16[2560,1280]{1,0:T(8,128)(2,1)} async-done(((bf16[160,1280]{1,0:T(8,128)(2,1)}), bf16[2560,1280]{1,0:T(8,128)(2,1)}) %all-gather.7.cloned.1.call-update) | async-done | bytes 6553616 | tf_op jit(solution)/shard_map/all_gather | solution.py:174
  148.3 5.6 %fusion.14 = f32[128,1280]{0,1:T(8,128)S(1)} fusion(bf16[2560,1280]{1,0:T(8,128)(2,1)} %all-gather.7.cloned.1.call-done, bf16[128,2560]{1,0:T(8,128)(2,1)S(1)} %all_gather.19, f32[128]{0:T(128)S(1)} %add_rsqrt_fusion), kind=kOutput, calls=%fused_computation.46 | convolution fusion | flops 839843840 | bytes 7864832 | tf_op jit(solution)/shard_map/dot_general | solution.py:92
  154.9 0.4 fusion.57
  155.3 0.5 fusion.56
  155.9 0.4 fusion.8
  156.3 0.5 fusion.10
  157.4 55.0 %all-gather.11.cloned.1.call-done = bf16[1280,2560]{0,1:T(8,128)(2,1)} async-done(((bf16[1280,160]{0,1:T(8,128)(2,1)}), bf16[1280,2560]{0,1:T(8,128)(2,1)}) %all-gather.11.cloned.1.call-update) | async-done | bytes 6553616 | tf_op jit(solution)/shard_map/all_gather | solution.py:120
  212.4 5.1 %convolution_convert_fusion = bf16[128,2560]{1,0:T(8,128)(2,1)S(1)} fusion(bf16[128,1280]{1,0:T(8,128)(2,1)S(1)} %bitcast.118, bf16[1280,2560]{0,1:T(8,128)(2,1)} %all-gather.11.cloned.1.call-done), kind=kOutput, calls=%fused_computation.5 | convolution fusion | flops 839188480 | bytes 7536640 | tf_op jit(solution)/shard_map/dot_general | solution.py:118
  217.5 0.3 copy.69
  217.8 0.9 copy.70
  219.0 0.3 fusion.6
  219.6 0.6 gather_fusion.4
  220.2 0.9 broadcast_select_fusion
  221.1 12.3 %reduce-scatter.2.cloned.1.call-done = bf16[128,1280]{0,1:T(8,128)(2,1)} async-done(((bf16[128,2560]{0,1:T(8,128)(2,1)}), bf16[128,1280]{0,1:T(8,128)(2,1)}) %reduce-scatter.2.cloned.1.call-update) | async-done | bytes 327696 | tf_op jit(solution)/shard_map/reduce_scatter | solution.py:129
  233.4 1.9 copy.72
  (89 shorter events, 5.9 us)
Async XLA Ops:
  7.2 39.3 %all-gather.5.cloned.1.call-start = ((), (), s32[]{:S(2)}) async-start(), calls=%async_computation.1 | async-start | bytes 1572864 | tf_op jit(solution)/shard_map/all_gather | solution.py:191
  7.9 75.4 %all-gather.9.cloned.1.call-start = ((), (), s32[]{:S(2)}) async-start(), calls=%async_computation.3 | async-start | bytes 2785280 | tf_op jit(solution)/shard_map/all_gather | solution.py:96
  8.6 139.6 %all-gather.7.cloned.1.call-start = ((), (), s32[]{:S(2)}) async-start(), calls=%async_computation.2 | async-start | bytes 6963200 | tf_op jit(solution)/shard_map/all_gather | solution.py:174
  10.7 1.1 copy-start.1
  11.6 200.8 %all-gather.11.cloned.1.call-start = ((), (), s32[]{:S(2)}) async-start(), calls=%async_computation.4 | async-start | bytes 6963200 | tf_op jit(solution)/shard_map/all_gather | solution.py:120
  30.0 1.0 copy-start.6
  30.0 3.0 %copy-start.4 = (s32[2]{0:T(128)S(1)}, s32[2]{0:T(128)}, u32[]{:S(2)}) copy-start(s32[2]{0:T(128)} %param.18) | copy-start | bytes 28
  30.0 3.6 %copy-start.5 = (s32[2,64]{1,0:T(2,128)S(1)}, s32[2,64]{1,0:T(2,128)}, u32[]{:S(2)}) copy-start(s32[2,64]{1,0:T(2,128)} %param.17) | copy-start | bytes 1540
  30.0 5.1 %copy-start.3 = (s32[2,4]{1,0:T(2,128)S(1)}, s32[2,4]{1,0:T(2,128)}, u32[]{:S(2)}) copy-start(s32[2,4]{1,0:T(2,128)} %param.16) | copy-start | bytes 100
  30.0 5.2 %copy-start = (bf16[4,2,128,256]{3,2,1,0:T(8,128)(2,1)S(1)}, bf16[4,2,128,256]{3,2,1,0:T(8,128)(2,1)}, u32[]{:S(2)}) copy-start(bf16[4,2,128,256]{3,2,1,0:T(8,128)(2,1)} %param.15) | copy-start | bytes 1572868
  30.9 202.6 %reduce-scatter.2.cloned.1.call-start = ((), (), s32[]{:S(2)}) async-start(), calls=%async_computation.5 | async-start | bytes 983040 | tf_op jit(solution)/shard_map/reduce_scatter | solution.py:129
  35.9 2.0 copy-start.2
Sparse Core Ops, SparseCore 0:
  9.5 26.7 all-gather.4
  38.6 44.6 all-gather.8
  86.2 62.0 all-gather.6
  150.4 61.9 all-gather.10
  218.9 14.5 reduce-scatter.1
where the time goes:
time: 242 us
  waiting for transfers between devices  166 us (69%)
  blocking collectives  25.8 us (11%)
  matrix products  16.6 us (7%)
  between operations  16.4 us (7%)
  local copies, waits for them, and re-layouts  12 us (5%)
  other arithmetic  5.35 us (2%)
    all_gather x1, waiting for transfers between devices, shards(): lax.all_gather(my_query_weight, 'tok', axis=0, tiled=True)  62.2 us
    all_gather x1, waiting for transfers between devices, reduce_heads(): lax.all_gather(my_output_weight, 'tok', axis=1, tiled=True)  55 us
    all_gather x1, waiting for transfers between devices, project_memory(): lax.all_gather(keyvalue_weight, 'tok', axis=0, tiled=True)  34.7 us
    all_gather x1, blocking collectives, reduce_heads(): blocks = lax.all_gather(output_weight, 'head', axis=1, tiled=True)  17.6 us
    reduce_scatter x1, waiting for transfers between devices, reduce_heads(): lax.psum_scatter(partial_value.astype(jnp.float32).astype(jnp.bfloat16),...  12.3 us
    all_gather x1, blocking collectives, shards(): gathered = lax.all_gather(tokens, 'head', axis=1, tiled=True)  8.21 us
    dot_general x2, matrix products, contract(): return jnp.dot(source, piece, preferred_element_type=jnp.float32)  7.87 us
    dot_general x1, matrix products, reduce_heads(): jnp.dot(mixed, lax.all_gather(my_output_weight, 'tok', axis=1, tiled=True...  5.1 us
  transfers between devices with their start and end apart: 5, of which 4 were waited for; matrix products, arithmetic and copies ran while one was open for 11% of the time, Pallas kernels for 0%

commit v1 on v0

--- a/solution.py
+++ b/solution.py
@@ -3,6 +3,8 @@
 import jax
 import jax.numpy as jnp
 from jax import lax
+from jax.experimental import pallas as pl
+from jax.experimental.pallas import tpu as pltpu
 from jax.sharding import PartitionSpec as P
 
 HQ = 10
@@ -11,6 +13,11 @@
 PAGE = 128
 NPR = 4
 WINDOW = 256
+CORES = 2
+XS = 2
+TILE = 16
+MESH = pl.DeviceIdType.MESH
+NT = (((1,), (1,)), ((), ()))
 
 
 def ancestry(parent_row):
@@ -224,6 +231,459 @@
     return (attended, cache_out)
 
 
+def fused_kernel(
+    tok_ref,
+    qw_ref,
+    kvw_ref,
+    wo_ref,
+    cache_ref,
+    parents_ref,
+    table_ref,
+    len_ref,
+    leaf_ref,
+    out_ref,
+    cache_out_ref,
+    wbuf,
+    obuf,
+    osend,
+    xbuf,
+    cbuf,
+    kvbuf,
+    qbuf,
+    mixbuf,
+    reach_buf,
+    depth_buf,
+    psend,
+    precv,
+    y_send,
+    y_recv,
+    *piece_sems,
+):
+    tok_count = wbuf.shape[0]
+    levels = tok_count // (XS * CORES)
+    slots = qbuf.shape[0]
+    rows = tok_ref.shape[0]
+    half = tok_ref.shape[1]
+    narrow = wo_ref.shape[0]
+    main_rows = narrow - TILE
+    requests = parents_ref.shape[0]
+    qcols = slots * HD
+    me = lax.axis_index("tok")
+    y = lax.axis_index("head")
+    other = 1 - y
+    core = lax.rem(me, CORES)
+    xpos = lax.rem(lax.div(me, CORES), XS)
+    z = lax.div(me, CORES * XS)
+
+    def tok_at(zz, xx, cc):
+        return (zz * XS + xx) * CORES + cc
+
+    up_dev = (jnp.minimum(me + XS * CORES, tok_count - 1), y)
+    down_dev = (jnp.maximum(me - XS * CORES, 0), y)
+    x_dev = (tok_at(z, 1 - xpos, core), y)
+    core_dev = (tok_at(z, xpos, 1 - core), y)
+    y_dev = (me, other)
+    has_up = z < levels - 1
+    has_down = z > 0
+
+    barrier = pltpu.get_barrier_semaphore()
+    for device in (x_dev, core_dev, y_dev):
+        pl.semaphore_signal(barrier, inc=1, device_id=device, device_id_type=MESH)
+
+    @pl.when(has_up)
+    def _():
+        pl.semaphore_signal(barrier, inc=1, device_id=up_dev, device_id_type=MESH)
+
+    @pl.when(has_down)
+    def _():
+        pl.semaphore_signal(barrier, inc=1, device_id=down_dev, device_id_type=MESH)
+
+    for slot in range(slots):
+        source = pl.ds(pl.multiple_of((2 * slot + y) * HD, HD), HD)
+        wbuf[me, :, slot * HD : (slot + 1) * HD] = qw_ref[:, source]
+    wbuf[me, :, qcols:] = kvw_ref[:, pl.ds(pl.multiple_of(y * HD, HD), HD)]
+
+    pl.semaphore_wait(barrier, 3 + has_up.astype(jnp.int32) + has_down.astype(jnp.int32))
+
+    def remote(source, target, send_sem, recv_sem, device):
+        return pltpu.make_async_remote_copy(
+            src_ref=source,
+            dst_ref=target,
+            send_sem=send_sem,
+            recv_sem=recv_sem,
+            device_id=device,
+            device_id_type=MESH,
+        )
+
+    class Piece:
+        def __init__(self, view, sems, x_first):
+            self.view = view
+            self.up, self.down, self.xs, self.cs, self.recv = sems
+            self.x_first = x_first
+
+        def copy(self, t, sems, device):
+            ref = self.view(t)
+            return remote(ref, ref, sems.at[lax.div(t, CORES)], self.recv.at[t], device)
+
+        def along(self, t, act, up, down):
+            if up:
+                pl.when(has_up)(lambda: act(self.copy(t, self.up, up_dev)))
+            if down:
+                pl.when(has_down)(lambda: act(self.copy(t, self.down, down_dev)))
+
+        def spread(self, t, distance, own_x, act):
+            if own_x and (not self.x_first or distance == 0):
+                act(self.copy(t, self.xs, x_dev))
+            act(self.copy(t, self.cs, core_dev))
+
+        def arrive(self, t):
+            self.copy(t, self.cs, core_dev).wait_recv()
+
+        def visit(self, distance, sending, act):
+            xs = (xpos, 1 - xpos) if self.x_first else (xpos,)
+            for order, xx in enumerate(xs):
+                if distance == 0:
+                    t = tok_at(z, xx, core)
+                    if sending and order == 1:
+                        self.arrive(t)
+                    self.along(t, act, True, True)
+                    self.spread(t, 0, order == 0, act)
+                    continue
+
+                @pl.when(z - distance >= 0)
+                def _():
+                    t = tok_at(z - distance, xx, core)
+                    if sending:
+                        self.arrive(t)
+                    self.along(t, act, True, False)
+                    self.spread(t, distance, order == 0, act)
+
+                @pl.when(z + distance < levels)
+                def _():
+                    t = tok_at(z + distance, xx, core)
+                    if sending:
+                        self.arrive(t)
+                    self.along(t, act, False, True)
+                    self.spread(t, distance, order == 0, act)
+
+        def cross(self, distance, sending, act):
+            if self.x_first:
+                return
+            targets = [z] if distance == 0 else [z - distance, z + distance]
+            for index, zz in enumerate(targets):
+
+                def go(zz=zz):
+                    t = tok_at(zz, 1 - xpos, core)
+                    if sending:
+                        self.arrive(t)
+                    self.spread(t, distance, False, act)
+
+                if distance == 0:
+                    go()
+                else:
+                    pl.when(zz >= 0 if index == 0 else zz < levels)(go)
+
+        def step(self, distance):
+            self.visit(distance, True, lambda copy: copy.start())
+
+        def relay(self, distance):
+            self.cross(distance, True, lambda copy: copy.start())
+
+        def finish(self):
+            for zz in range(levels):
+                for xx in range(XS):
+                    self.arrive(tok_at(zz, xx, 1 - core))
+
+        def drain(self):
+            for distance in range(levels):
+                self.visit(distance, False, lambda copy: copy.wait_send())
+                self.cross(distance, False, lambda copy: copy.wait_send())
+
+    pieces = [piece_sems[5 * i : 5 * i + 5] for i in range(4)]
+    q_piece = Piece(lambda t: wbuf.at[t, :, :qcols], pieces[0], False)
+    k_piece = Piece(lambda t: wbuf.at[t, :, qcols:], pieces[1], True)
+    o_piece = Piece(lambda t: obuf.at[:, t, :main_rows], pieces[2], False)
+    s_piece = Piece(lambda t: obuf.at[:, t, main_rows:], pieces[3], True)
+
+    def step(group, distance):
+        for piece in group:
+            piece.step(distance)
+
+    def relay(group, distance):
+        for piece in group:
+            piece.relay(distance)
+
+    weights = (q_piece, k_piece)
+    outputs = (o_piece, s_piece)
+
+    q_piece.step(0)
+
+    xsend = remote(tok_ref, xbuf.at[y], y_send.at[0], y_recv.at[0], y_dev)
+    xsend.start()
+    for slot in range(slots):
+        source = pl.ds(pl.multiple_of((2 * slot + other) * HD, HD), HD)
+        osend[:, slot * HD : (slot + 1) * HD] = wo_ref[:, source]
+    wosend = remote(osend, obuf.at[y, me], y_send.at[1], y_recv.at[1], y_dev)
+    wosend.start()
+    csend = remote(cache_ref, cbuf.at[y], y_send.at[2], y_recv.at[2], y_dev)
+    csend.start()
+    for slot in range(slots):
+        source = pl.ds(pl.multiple_of((2 * slot + y) * HD, HD), HD)
+        obuf[y, me, :, slot * HD : (slot + 1) * HD] = wo_ref[:, source]
+    xbuf[y] = tok_ref[...]
+    cbuf[y] = cache_ref[...]
+
+    k_piece.step(0)
+
+    row_ids = lax.broadcasted_iota(jnp.int32, (DRAFT, DRAFT), 0)
+    col_ids = lax.broadcasted_iota(jnp.int32, (DRAFT, DRAFT), 1)
+    eye = (row_ids == col_ids).astype(jnp.float32)
+    lane = lax.broadcasted_iota(jnp.int32, (1, HD // 2), 1)
+    quarter = HD // 4
+    pair = jnp.where(lane < quarter, lane, lane - quarter).astype(jnp.float32)
+    freq = jnp.exp(pair * (-2.0 * math.log(10000.0) / (HD // 2)))
+    sign = jnp.where(lane < quarter, -1.0, 1.0)
+    reaches = []
+    positions = []
+    for r in range(requests):
+        back = (row_ids == parents_ref[r : r + 1, :]).astype(jnp.float32)
+        back = jnp.minimum(back + eye, 1.0)
+        for sweep in range((DRAFT - 1).bit_length()):
+            low = back.astype(jnp.bfloat16)
+            back = jnp.minimum(jnp.dot(low, low, preferred_element_type=jnp.float32), 1.0)
+        reach = lax.dot_general(
+            eye.astype(jnp.bfloat16),
+            back.astype(jnp.bfloat16),
+            NT,
+            preferred_element_type=jnp.float32,
+        )
+        reach_buf[r] = reach
+        depth_buf[r] = jnp.sum(back, axis=0, keepdims=True) - 1.0
+        reaches.append(reach)
+        depth = jnp.sum(reach, axis=1, keepdims=True) - 1.0
+        positions.append(depth + len_ref[r].astype(jnp.float32))
+    angle = jnp.concatenate(positions, axis=0) * freq
+    cosine = jnp.cos(angle)
+    sine = jnp.sin(angle) * sign
+
+    def rotated(value):
+        turn = value[:, : HD // 2]
+        swapped = jnp.concatenate([turn[:, quarter:], turn[:, :quarter]], axis=1)
+        return jnp.concatenate([turn * cosine + swapped * sine, value[:, HD // 2 :]], axis=1)
+
+    step(weights, 1)
+    relay(weights, 0)
+    xsend.wait_recv()
+    wide = jnp.concatenate([xbuf[0], xbuf[1]], axis=1).astype(jnp.float32)
+    mean_square = jnp.mean(wide * wide, axis=1, keepdims=True)
+    normed = (wide * lax.rsqrt(mean_square + 1e-06)).astype(jnp.bfloat16)
+
+    for distance in range(2, levels):
+        step(weights, distance)
+        relay(weights, distance - 1)
+        if distance == 2:
+            wosend.wait_recv()
+            step(outputs, 0)
+    step(outputs, 1)
+    relay(weights, levels - 1)
+    for piece in weights:
+        piece.finish()
+
+    def project(start):
+        block = wbuf[:, :, start : start + HD].reshape(-1, HD)
+        return jnp.dot(normed, block, preferred_element_type=jnp.float32)
+
+    projected = project(qcols)
+
+    @pl.when(y == 0)
+    def _():
+        kvbuf[0] = rotated(projected).astype(jnp.bfloat16)
+
+    @pl.when(y == 1)
+    def _():
+        kvbuf[1] = projected.astype(jnp.bfloat16)
+
+    kvsend = remote(kvbuf.at[y], kvbuf.at[y], y_send.at[3], y_recv.at[3], y_dev)
+    kvsend.start()
+    for slot in range(slots):
+        qbuf[slot] = (rotated(project(slot * HD)) * HD ** (-0.5)).astype(jnp.bfloat16)
+    relay(outputs, 0)
+    kvsend.wait_recv()
+    csend.wait_recv()
+
+    def attend_one(r):
+        span = slice(r * DRAFT, (r + 1) * DRAFT)
+        queries = qbuf[:, span, :].reshape(slots * DRAFT, HD)
+        ids = [lax.rem(table_ref[r, j], NPR) for j in range(NPR)]
+        keys = jnp.concatenate([cbuf[r, i, 0] for i in ids], axis=0)
+        values = jnp.concatenate([cbuf[r, i, 1] for i in ids], axis=0)
+        span_len = NPR * PAGE
+        slot_ids = lax.broadcasted_iota(jnp.int32, (DRAFT, span_len), 1)
+        first = positions[r].astype(jnp.int32) - WINDOW
+        visible = (slot_ids < len_ref[r]) & (slot_ids > first)
+        cache_bias = jnp.where(visible, 0.0, -1e30)
+        tree_bias = jnp.where(reaches[r] > 0.5, 0.0, -1e30)
+        scores = lax.dot_general(queries, keys, NT, preferred_element_type=jnp.float32)
+        tree = lax.dot_general(queries, kvbuf[0, span, :], NT, preferred_element_type=jnp.float32)
+        scores = jnp.where(cache_bias[None] < 0.0, -1e30, scores.reshape(slots, DRAFT, span_len))
+        tree = jnp.where(tree_bias[None] < 0.0, -1e30, tree.reshape(slots, DRAFT, DRAFT))
+        peak = jnp.maximum(
+            jnp.max(scores, axis=-1, keepdims=True), jnp.max(tree, axis=-1, keepdims=True)
+        )
+        scores = jnp.exp(scores - peak)
+        tree = jnp.exp(tree - peak)
+        total = jnp.sum(scores, axis=-1, keepdims=True) + jnp.sum(tree, axis=-1, keepdims=True)
+        scores = (scores / total).astype(jnp.bfloat16).reshape(slots * DRAFT, span_len)
+        tree = (tree / total).astype(jnp.bfloat16).reshape(slots * DRAFT, DRAFT)
+        result = jnp.dot(scores, values, preferred_element_type=jnp.float32)
+        result = result + jnp.dot(tree, kvbuf[1, span, :], preferred_element_type=jnp.float32)
+        result = result.astype(jnp.bfloat16)
+        for slot in range(slots):
+            mixbuf[span, slot * HD : (slot + 1) * HD] = result[slot * DRAFT : (slot + 1) * DRAFT]
+
+    def refresh_one():
+        length = len_ref[y]
+        own_reach = reach_buf[y]
+        on_path = jnp.sum(jnp.where(row_ids == leaf_ref[y], own_reach, 0.0), axis=0, keepdims=True)
+        depth_row = depth_buf[y].astype(jnp.int32)
+        keep = pl.ds(pl.multiple_of(y * DRAFT, DRAFT), DRAFT)
+        new_keys = kvbuf[0, keep, :]
+        new_values = kvbuf[1, keep, :]
+        slot_ids = lax.broadcasted_iota(jnp.int32, (PAGE, DRAFT), 0)
+        for page in range(NPR):
+            logical = jnp.int32(0)
+            for j in range(1, NPR):
+                logical = logical + jnp.where(lax.rem(table_ref[y, j], NPR) == page, j, 0)
+            chosen = (on_path > 0.5) & (depth_row == slot_ids + (logical * PAGE - length))
+            selector = chosen.astype(jnp.float32)
+            written = jnp.sum(selector, axis=1, keepdims=True) > 0.5
+            selector = selector.astype(jnp.bfloat16)
+            for entry, new in ((0, new_keys), (1, new_values)):
+                placed = jnp.dot(selector, new, preferred_element_type=jnp.float32)
+                old = cache_ref[page, entry].astype(jnp.float32)
+                cache_out_ref[page, entry] = jnp.where(written, placed, old).astype(jnp.bfloat16)
+
+    step(outputs, 2) if levels > 2 else None
+    relay(outputs, 1)
+    attend_one(0)
+    for distance in range(3, levels):
+        step(outputs, distance)
+        relay(outputs, distance - 1)
+    for r in range(1, requests):
+        attend_one(r)
+    refresh_one()
+    relay(outputs, levels - 1)
+    for piece in outputs:
+        piece.finish()
+
+    mixed = mixbuf[...]
+    part = tok_count // 2
+    width = part * narrow
+    sends = []
+    for index in range(2):
+        block = obuf[other, index * part : (index + 1) * part].reshape(width, qcols)
+        value = lax.dot_general(mixed, block, NT, preferred_element_type=jnp.float32)
+        psend[index] = value.astype(jnp.bfloat16)
+        copy = remote(
+            psend.at[index], precv.at[index], y_send.at[4 + index], y_recv.at[4 + index], y_dev
+        )
+        copy.start()
+        sends.append(copy)
+    for index in range(2):
+        block = obuf[y, index * part : (index + 1) * part].reshape(width, qcols)
+        value = lax.dot_general(mixed, block, NT, preferred_element_type=jnp.float32)
+        value = value.astype(jnp.bfloat16).astype(jnp.float32)
+        sends[index].wait_recv()
+        summed = value + precv[index].astype(jnp.float32)
+        out_ref[:, index * width : (index + 1) * width] = summed.astype(jnp.bfloat16)
+    for piece in weights + outputs:
+        piece.drain()
+    for copy in [xsend, wosend, csend, kvsend] + sends:
+        copy.wait_send()
+
+
+def fused(tokens, query_weight, keyvalue_weight, output_weight, cache, page_table, parents, cache_len, accepted_leaf):
+    tok_count = lax.axis_size("tok")
+    heads = lax.axis_size("head")
+    slots = HQ // heads
+    rows, half = tokens.shape
+    part_rows = query_weight.shape[0]
+    narrow = output_weight.shape[1]
+    requests = parents.shape[0]
+    pages = cache.shape[0]
+    qcols = slots * HD
+    positions = tok_count // CORES
+    vmem = pl.BlockSpec(memory_space=pltpu.VMEM)
+    smem = pl.BlockSpec(memory_space=pltpu.SMEM)
+    bf16 = jnp.bfloat16
+    scratch = [
+        pltpu.VMEM((tok_count, part_rows, qcols + HD), bf16),
+        pltpu.VMEM((heads, tok_count, narrow, qcols), bf16),
+        pltpu.VMEM((narrow, qcols), bf16),
+        pltpu.VMEM((heads, rows, half), bf16),
+        pltpu.VMEM((heads,) + cache.shape, bf16),
+        pltpu.VMEM((2, rows, HD), bf16),
+        pltpu.VMEM((slots, rows, HD), bf16),
+        pltpu.VMEM((rows, qcols), bf16),
+        pltpu.VMEM((requests, DRAFT, DRAFT), jnp.float32),
+        pltpu.VMEM((requests, 1, DRAFT), jnp.float32),
+        pltpu.VMEM((2, rows, half // 2), bf16),
+        pltpu.VMEM((2, rows, half // 2), bf16),
+        pltpu.SemaphoreType.DMA((6,)),
+        pltpu.SemaphoreType.DMA((6,)),
+    ]
+    for piece in range(4):
+        scratch += [pltpu.SemaphoreType.DMA((positions,))] * 4
+        scratch += [pltpu.SemaphoreType.DMA((tok_count,))]
+    return pl.pallas_call(
+        fused_kernel,
+        out_shape=(
+            jax.ShapeDtypeStruct(tokens.shape, bf16),
+            jax.ShapeDtypeStruct(cache.shape, bf16),
+        ),
+        in_specs=[vmem] * 6 + [smem] * 3,
+        out_specs=(vmem, vmem),
+        scratch_shapes=scratch,
+        compiler_params=pltpu.CompilerParams(
+            collective_id=0, has_side_effects=True, vmem_limit_bytes=48 * 1024 * 1024
+        ),
+        cost_estimate=pl.CostEstimate(
+            flops=4 * rows * HD * HQ * HD * 5, bytes_accessed=1 << 22, transcendentals=1 << 19
+        ),
+    )(
+        tokens,
+        query_weight,
+        keyvalue_weight,
+        jnp.transpose(output_weight),
+        cache,
+        parents,
+        page_table,
+        cache_len,
+        accepted_leaf,
+    )
+
+
+def fits(tok_count, head_count, args):
+    tokens, query_weight, _, output_weight, cache, _, parents, _, _ = args
+    return (
+        head_count == 2
+        and tok_count % (2 * XS * CORES) == 0
+        and tok_count >= 3 * XS * CORES
+        and query_weight.shape[0] % TILE == 0
+        and output_weight.shape[1] % TILE == 0
+        and output_weight.shape[1] > TILE
+        and (tokens.shape[1] // 2) % 128 == 0
+        and cache.shape[0] == NPR
+        and parents.shape[0] == head_count
+    )
+
+
+def dispatch(*args):
+    if fits(lax.axis_size("tok"), lax.axis_size("head"), args):
+        return fused(*args)
+    return shards(*args)
+
+
 def solution(mesh):
     in_specs = (
         P("tok", "head"),
@@ -237,4 +697,6 @@
         P("tok"),
     )
     out_specs = (P("tok", "head"), P(("tok", "head"), None, None, None))
-    return jax.shard_map(shards, mesh=mesh, in_specs=in_specs, out_specs=out_specs, check_vma=False)
+    return jax.shard_map(
+        dispatch, mesh=mesh, in_specs=in_specs, out_specs=out_specs, check_vma=False
+    )

time: 242 us -> 104 us (0.43)
  waiting for transfers between devices: 166 us -> 0 us
  Pallas kernels: 0 us -> 93.7 us
  blocking collectives: 25.8 us -> 0 us
  matrix products: 16.6 us -> 0 us
  between operations: 16.4 us -> 0.67 us
  other arithmetic: 5.35 us -> 0 us
  local copies, waits for them, and re-layouts: 12 us -> 8.61 us
    all_gather x4 -> x0, waiting for transfers between devices: 152 us -> none  [the longest x1 62.2 us: shards(): lax.all_gather(my_query_weight, 'tok', axis=0, tiled=True)]
    pallas_call x0 -> x1, Pallas kernels: none -> 93.7 us  [fused(): pl.pallas_call(fused_kernel, out_shape=(jax.ShapeDtypeStruct(tokens.shape...]
    all_gather x2 -> x0, blocking collectives: 25.8 us -> none  [the longest x1 17.6 us: reduce_heads(): blocks = lax.all_gather(output_weight, 'head', axis=1, tiled=True)]
    dot_general x15 -> x0, matrix products: 16.6 us -> none  [the longest x2 7.87 us: contract(): return jnp.dot(source, piece, preferred_element_type=jnp.float32)]
    reduce_scatter x1 -> x0, waiting for transfers between devices: 12.3 us -> none  [reduce_heads(): lax.psum_scatter(partial_value.astype(jnp.float32).astype(jnp.bfloat16),...]
    unnamed x16 -> x20, local copies, waits for them, and re-layouts: 2.12 us -> 8.61 us
    gather x7 -> x0, local copies, waits for them, and re-layouts: 4.22 us -> none  [the longest x1 1.86 us: shards(): jnp.take(page_pool, local_ids.reshape(-1), axis=0)]
  transfers between devices with their start and end apart: 5 -> 0, of which waited for: 4 -> 0; matrix products, arithmetic and copies ran while one was open for 11% -> 0% of each run, Pallas kernels for 0% -> 0%
where the time goes in v1:
time: 104 us; the launch traced here: 103 us
  Pallas kernels  93.7 us (90%)
  local copies, waits for them, and re-layouts  8.61 us (8%)
    pallas_call x1, Pallas kernels, fused(): pl.pallas_call(fused_kernel, out_shape=(jax.ShapeDtypeStruct(tokens.shape...  93.7 us
    unnamed x20, local copies, waits for them, and re-layouts  8.61 us

profile of v1, /device:TPU:0, one launch (start us, length us, event | category | flops | bytes accessed | tf_op | source)
XLA Modules:
  0.0 103.0 jit_solution(17808415240237624413)
XLA Ops:
  0.6 0.0 copy-start.7
  0.6 0.0 copy-start.5
  0.7 0.6 copy-done.7
  1.3 0.0 copy-done.5
  1.3 0.0 copy-start
  1.3 1.1 %copy-done = bf16[160,2560]{1,0:T(8,128)(2,1)S(1)} copy-done((bf16[160,2560]{1,0:T(8,128)(2,1)S(1)}, bf16[160,2560]{1,0:T(8,128)(2,1)}, u32[]{:S(2)}) %copy-start) | copy-done | bytes 819224
  2.5 0.0 copy-start.1
  2.5 1.0 %copy-done.1 = bf16[4,2,128,256]{3,2,1,0:T(8,128)(2,1)S(1)} copy-done((bf16[4,2,128,256]{3,2,1,0:T(8,128)(2,1)S(1)}, bf16[4,2,128,256]{3,2,1,0:T(8,128)(2,1)}, u32[]{:S(2)}) %copy-start.1) | copy-done | bytes 524312
  3.5 0.0 copy-start.2
  3.5 1.0 copy-done.2
  4.5 0.0 copy-start.3
  4.5 1.0 copy-done.3
  5.5 0.0 copy-start.4
  5.5 0.9 copy-done.4
  6.4 0.0 copy-start.6
  6.4 0.7 copy-done.6
  7.1 0.0 copy-start.8
  7.1 0.7 copy-done.8
  7.7 93.7 %shard_map.104 = (bf16[128,1280]{1,0:T(8,128)(2,1)S(1)}, bf16[4,2,128,256]{3,2,1,0:T(8,128)(2,1)S(1)}) custom-call(bf16[128,1280]{1,0:T(8,128)(2,1)S(1)} %copy-done.3, bf16[160,2560]{1,0:T(8,128)(2,1)S(1)} %copy-done, bf16[160,512]{1,0:T(8,128)(2,1)S(1)} %copy-done.4, bf16[80,2560]{1,0:T(8,128)(2,1)S(1)} %bitcast.1, bf16[4,2,128,256]{3,2,1,0:T(8,128)(2,1)S(1)} %copy-done.1, ...), custom_call_target="tpu_custom_call" | custom-call | flops 1677721600 | bytes 4194304 | tf_op jit(solution)/shard_map/pallas_call | solution.py:638
  101.5 0.7 copy.13
  102.2 0.8 copy.14
Async XLA Ops:
  0.6 0.7 copy-start.7
  0.6 0.7 copy-start.5
  1.3 1.1 %copy-start = (bf16[160,2560]{1,0:T(8,128)(2,1)S(1)}, bf16[160,2560]{1,0:T(8,128)(2,1)}, u32[]{:S(2)}) copy-start(bf16[160,2560]{1,0:T(8,128)(2,1)} %qw_ref.1) | copy-start | bytes 2457604
  2.5 1.0 %copy-start.1 = (bf16[4,2,128,256]{3,2,1,0:T(8,128)(2,1)S(1)}, bf16[4,2,128,256]{3,2,1,0:T(8,128)(2,1)}, u32[]{:S(2)}) copy-start(bf16[4,2,128,256]{3,2,1,0:T(8,128)(2,1)} %cache_ref.1) | copy-start | bytes 1572868
  3.5 1.0 copy-start.2
  4.5 1.0 copy-start.3
  5.5 0.9 copy-start.4
  6.4 0.7 copy-start.6
  7.1 0.7 copy-start.8

commit v2 on v1

--- a/solution.py
+++ b/solution.py
@@ -245,7 +245,6 @@
     cache_out_ref,
     wbuf,
     obuf,
-    osend,
     xbuf,
     cbuf,
     kvbuf,
@@ -253,20 +252,27 @@
     mixbuf,
     reach_buf,
     depth_buf,
+    nbuf,
+    accum,
     psend,
+    pown,
     precv,
     y_send,
     y_recv,
+    part_send,
+    part_recv,
+    load_sem,
     *piece_sems,
 ):
     tok_count = wbuf.shape[0]
     levels = tok_count // (XS * CORES)
     slots = qbuf.shape[0]
     rows = tok_ref.shape[0]
-    half = tok_ref.shape[1]
     narrow = wo_ref.shape[0]
     main_rows = narrow - TILE
     requests = parents_ref.shape[0]
+    level = XS * CORES
+    part_rows = wbuf.shape[1]
     qcols = slots * HD
     me = lax.axis_index("tok")
     y = lax.axis_index("head")
@@ -286,6 +292,33 @@
     has_up = z < levels - 1
     has_down = z > 0
 
+    def columns(slot, group):
+        return pl.ds(pl.multiple_of((2 * slot + group) * HD, HD), HD)
+
+    loads = [
+        (
+            qw_ref.at[:, columns(slot, y)],
+            wbuf.at[me, :, slot * HD : (slot + 1) * HD],
+        )
+        for slot in range(slots)
+    ]
+    loads.append((kvw_ref.at[:, pl.ds(pl.multiple_of(y * HD, HD), HD)], wbuf.at[me, :, qcols:]))
+    weight_loads = len(loads)
+    loads += [
+        (
+            wo_ref.at[:, columns(slot, y)],
+            obuf.at[y, me, :, slot * HD : (slot + 1) * HD],
+        )
+        for slot in range(slots)
+    ]
+    loads += [(tok_ref, xbuf.at[y]), (cache_ref, cbuf.at[y])]
+    loads = [
+        pltpu.make_async_copy(source, target, load_sem.at[index])
+        for index, (source, target) in enumerate(loads)
+    ]
+    for load in loads:
+        load.start()
+
     barrier = pltpu.get_barrier_semaphore()
     for device in (x_dev, core_dev, y_dev):
         pl.semaphore_signal(barrier, inc=1, device_id=device, device_id_type=MESH)
@@ -297,11 +330,6 @@
     @pl.when(has_down)
     def _():
         pl.semaphore_signal(barrier, inc=1, device_id=down_dev, device_id_type=MESH)
-
-    for slot in range(slots):
-        source = pl.ds(pl.multiple_of((2 * slot + y) * HD, HD), HD)
-        wbuf[me, :, slot * HD : (slot + 1) * HD] = qw_ref[:, source]
-    wbuf[me, :, qcols:] = kvw_ref[:, pl.ds(pl.multiple_of(y * HD, HD), HD)]
 
     pl.semaphore_wait(barrier, 3 + has_up.astype(jnp.int32) + has_down.astype(jnp.int32))
 
@@ -339,9 +367,11 @@
         def arrive(self, t):
             self.copy(t, self.cs, core_dev).wait_recv()
 
-        def visit(self, distance, sending, act):
+        def visit(self, distance, sending, act, orders=(0, 1)):
             xs = (xpos, 1 - xpos) if self.x_first else (xpos,)
             for order, xx in enumerate(xs):
+                if order not in orders:
+                    continue
                 if distance == 0:
                     t = tok_at(z, xx, core)
                     if sending and order == 1:
@@ -383,27 +413,30 @@
                 else:
                     pl.when(zz >= 0 if index == 0 else zz < levels)(go)
 
-        def step(self, distance):
-            self.visit(distance, True, lambda copy: copy.start())
+        def step(self, distance, orders=(0, 1)):
+            self.visit(distance, True, lambda copy: copy.start(), orders)
 
         def relay(self, distance):
             self.cross(distance, True, lambda copy: copy.start())
 
-        def finish(self):
-            for zz in range(levels):
-                for xx in range(XS):
-                    self.arrive(tok_at(zz, xx, 1 - core))
+        def gathered(self, zz):
+            for xx in range(XS):
+                self.arrive(tok_at(zz, xx, 1 - core))
 
         def drain(self):
             for distance in range(levels):
                 self.visit(distance, False, lambda copy: copy.wait_send())
                 self.cross(distance, False, lambda copy: copy.wait_send())
 
-    pieces = [piece_sems[5 * i : 5 * i + 5] for i in range(4)]
-    q_piece = Piece(lambda t: wbuf.at[t, :, :qcols], pieces[0], False)
-    k_piece = Piece(lambda t: wbuf.at[t, :, qcols:], pieces[1], True)
-    o_piece = Piece(lambda t: obuf.at[:, t, :main_rows], pieces[2], False)
-    s_piece = Piece(lambda t: obuf.at[:, t, main_rows:], pieces[3], True)
+    pieces = [piece_sems[5 * i : 5 * i + 5] for i in range(6)]
+    cut = slots // 2 * HD
+    mid = main_rows // 2 // TILE * TILE
+    k_piece = Piece(lambda t: wbuf.at[t, :, qcols:], pieces[0], True)
+    qa_piece = Piece(lambda t: wbuf.at[t, :, :cut], pieces[1], False)
+    qb_piece = Piece(lambda t: wbuf.at[t, :, cut:qcols], pieces[2], False)
+    oa_piece = Piece(lambda t: obuf.at[:, t, :mid], pieces[3], False)
+    ob_piece = Piece(lambda t: obuf.at[:, t, mid:main_rows], pieces[4], False)
+    s_piece = Piece(lambda t: obuf.at[:, t, main_rows:], pieces[5], True)
 
     def step(group, distance):
         for piece in group:
@@ -413,27 +446,42 @@
         for piece in group:
             piece.relay(distance)
 
-    weights = (q_piece, k_piece)
-    outputs = (o_piece, s_piece)
-
-    q_piece.step(0)
-
+    def each_level(distance, run):
+        if distance == 0:
+            run(z)
+            return
+        pl.when(z - distance >= 0)(lambda: run(z - distance))
+        pl.when(z + distance < levels)(lambda: run(z + distance))
+
+    weights = (k_piece, qa_piece, qb_piece)
+    outputs = (oa_piece, ob_piece, s_piece)
+
+    wosends = [
+        remote(
+            wo_ref.at[:, columns(slot, other)],
+            obuf.at[y, me, :, slot * HD : (slot + 1) * HD],
+            y_send.at[3 + slot],
+            y_recv.at[3 + slot],
+            y_dev,
+        )
+        for slot in range(slots)
+    ]
     xsend = remote(tok_ref, xbuf.at[y], y_send.at[0], y_recv.at[0], y_dev)
-    xsend.start()
-    for slot in range(slots):
-        source = pl.ds(pl.multiple_of((2 * slot + other) * HD, HD), HD)
-        osend[:, slot * HD : (slot + 1) * HD] = wo_ref[:, source]
-    wosend = remote(osend, obuf.at[y, me], y_send.at[1], y_recv.at[1], y_dev)
-    wosend.start()
-    csend = remote(cache_ref, cbuf.at[y], y_send.at[2], y_recv.at[2], y_dev)
+    csend = remote(cache_ref, cbuf.at[y], y_send.at[1], y_recv.at[1], y_dev)
+    for copy in wosends + [xsend]:
+        copy.start()
+    for load in loads[:weight_loads]:
+        load.wait()
+    k_piece.step(0, (0,))
+    qa_piece.step(0)
+    qb_piece.step(0)
     csend.start()
-    for slot in range(slots):
-        source = pl.ds(pl.multiple_of((2 * slot + y) * HD, HD), HD)
-        obuf[y, me, :, slot * HD : (slot + 1) * HD] = wo_ref[:, source]
-    xbuf[y] = tok_ref[...]
-    cbuf[y] = cache_ref[...]
-
-    k_piece.step(0)
+    for load in loads[weight_loads:]:
+        load.wait()
+    k_piece.step(0, (1,))
+    for copy in wosends:
+        copy.wait_recv()
+    s_piece.step(0, (0,))
 
     row_ids = lax.broadcasted_iota(jnp.int32, (DRAFT, DRAFT), 0)
     col_ids = lax.broadcasted_iota(jnp.int32, (DRAFT, DRAFT), 1)
@@ -471,29 +519,48 @@
         swapped = jnp.concatenate([turn[:, quarter:], turn[:, :quarter]], axis=1)
         return jnp.concatenate([turn * cosine + swapped * sine, value[:, HD // 2 :]], axis=1)
 
-    step(weights, 1)
-    relay(weights, 0)
     xsend.wait_recv()
     wide = jnp.concatenate([xbuf[0], xbuf[1]], axis=1).astype(jnp.float32)
     mean_square = jnp.mean(wide * wide, axis=1, keepdims=True)
-    normed = (wide * lax.rsqrt(mean_square + 1e-06)).astype(jnp.bfloat16)
-
-    for distance in range(2, levels):
+    nbuf[...] = (wide * lax.rsqrt(mean_square + 1e-06)).astype(jnp.bfloat16)
+    span_rows = level * part_rows
+
+    def project(distance):
+        def run(zz):
+            for piece in weights:
+                piece.gathered(zz)
+            source = nbuf[:, pl.ds(pl.multiple_of(zz * span_rows, 128), span_rows)]
+            for slot in range(slots + 1):
+                at = slice(slot * HD, (slot + 1) * HD)
+                block = wbuf[pl.ds(zz * level, level), :, at].reshape(span_rows, HD)
+                part = jnp.dot(source, block, preferred_element_type=jnp.float32)
+                if distance == 0:
+                    accum[:, at] = part
+                else:
+                    accum[:, at] += part
+
+        each_level(distance, run)
+
+    step(weights, 1)
+    relay(weights, 0)
+    s_piece.step(0, (1,))
+    project(0)
+    step(weights, 2)
+    relay(weights, 1)
+    oa_piece.step(0)
+    ob_piece.step(0)
+    project(1)
+    for distance in range(3, levels):
         step(weights, distance)
         relay(weights, distance - 1)
-        if distance == 2:
-            wosend.wait_recv()
-            step(outputs, 0)
-    step(outputs, 1)
+        if distance == 3:
+            step(outputs, 1)
+        project(distance - 1)
+    relay(outputs, 0)
     relay(weights, levels - 1)
-    for piece in weights:
-        piece.finish()
-
-    def project(start):
-        block = wbuf[:, :, start : start + HD].reshape(-1, HD)
-        return jnp.dot(normed, block, preferred_element_type=jnp.float32)
-
-    projected = project(qcols)
+    project(levels - 1)
+
+    projected = accum[:, qcols:]
 
     @pl.when(y == 0)
     def _():
@@ -503,11 +570,13 @@
     def _():
         kvbuf[1] = projected.astype(jnp.bfloat16)
 
-    kvsend = remote(kvbuf.at[y], kvbuf.at[y], y_send.at[3], y_recv.at[3], y_dev)
+    kvsend = remote(kvbuf.at[y], kvbuf.at[y], y_send.at[2], y_recv.at[2], y_dev)
     kvsend.start()
+    step(outputs, 2)
+    relay(outputs, 1)
     for slot in range(slots):
-        qbuf[slot] = (rotated(project(slot * HD)) * HD ** (-0.5)).astype(jnp.bfloat16)
-    relay(outputs, 0)
+        value = rotated(accum[:, slot * HD : (slot + 1) * HD])
+        qbuf[slot] = (value * HD ** (-0.5)).astype(jnp.bfloat16)
     kvsend.wait_recv()
     csend.wait_recv()
 
@@ -560,45 +629,45 @@
             selector = selector.astype(jnp.bfloat16)
             for entry, new in ((0, new_keys), (1, new_values)):
                 placed = jnp.dot(selector, new, preferred_element_type=jnp.float32)
-                old = cache_ref[page, entry].astype(jnp.float32)
+                old = cbuf[y, page, entry].astype(jnp.float32)
                 cache_out_ref[page, entry] = jnp.where(written, placed, old).astype(jnp.bfloat16)
 
-    step(outputs, 2) if levels > 2 else None
-    relay(outputs, 1)
+    width = level * narrow
+
+    def part_copy(zz):
+        return remote(psend.at[zz], precv.at[zz], part_send.at[zz], part_recv.at[zz], y_dev)
+
+    def output_level(zz):
+        for piece in outputs:
+            piece.gathered(zz)
+        mixed = mixbuf[...]
+        block = obuf[other, pl.ds(zz * level, level)].reshape(width, qcols)
+        value = lax.dot_general(mixed, block, NT, preferred_element_type=jnp.float32)
+        psend[zz] = value.astype(jnp.bfloat16)
+        part_copy(zz).start()
+        block = obuf[y, pl.ds(zz * level, level)].reshape(width, qcols)
+        value = lax.dot_general(mixed, block, NT, preferred_element_type=jnp.float32)
+        pown[zz] = value.astype(jnp.bfloat16)
+
     attend_one(0)
     for distance in range(3, levels):
         step(outputs, distance)
         relay(outputs, distance - 1)
     for r in range(1, requests):
         attend_one(r)
+    for distance in range(levels - 1):
+        each_level(distance, output_level)
     refresh_one()
     relay(outputs, levels - 1)
-    for piece in outputs:
-        piece.finish()
-
-    mixed = mixbuf[...]
-    part = tok_count // 2
-    width = part * narrow
-    sends = []
-    for index in range(2):
-        block = obuf[other, index * part : (index + 1) * part].reshape(width, qcols)
-        value = lax.dot_general(mixed, block, NT, preferred_element_type=jnp.float32)
-        psend[index] = value.astype(jnp.bfloat16)
-        copy = remote(
-            psend.at[index], precv.at[index], y_send.at[4 + index], y_recv.at[4 + index], y_dev
-        )
-        copy.start()
-        sends.append(copy)
-    for index in range(2):
-        block = obuf[y, index * part : (index + 1) * part].reshape(width, qcols)
-        value = lax.dot_general(mixed, block, NT, preferred_element_type=jnp.float32)
-        value = value.astype(jnp.bfloat16).astype(jnp.float32)
-        sends[index].wait_recv()
-        summed = value + precv[index].astype(jnp.float32)
-        out_ref[:, index * width : (index + 1) * width] = summed.astype(jnp.bfloat16)
+    each_level(levels - 1, output_level)
+    sums = []
+    for zz in range(levels):
+        part_copy(zz).wait_recv()
+        sums.append(pown[zz].astype(jnp.float32) + precv[zz].astype(jnp.float32))
+    out_ref[...] = jnp.concatenate(sums, axis=1).astype(jnp.bfloat16)
     for piece in weights + outputs:
         piece.drain()
-    for copy in [xsend, wosend, csend, kvsend] + sends:
+    for copy in [xsend, csend, kvsend] + wosends + [part_copy(zz) for zz in range(levels)]:
         copy.wait_send()
 
 
@@ -613,13 +682,14 @@
     pages = cache.shape[0]
     qcols = slots * HD
     positions = tok_count // CORES
+    levels = positions // XS
+    hbm = pl.BlockSpec(memory_space=pl.ANY)
     vmem = pl.BlockSpec(memory_space=pltpu.VMEM)
     smem = pl.BlockSpec(memory_space=pltpu.SMEM)
     bf16 = jnp.bfloat16
     scratch = [
         pltpu.VMEM((tok_count, part_rows, qcols + HD), bf16),
         pltpu.VMEM((heads, tok_count, narrow, qcols), bf16),
-        pltpu.VMEM((narrow, qcols), bf16),
         pltpu.VMEM((heads, rows, half), bf16),
         pltpu.VMEM((heads,) + cache.shape, bf16),
         pltpu.VMEM((2, rows, HD), bf16),
@@ -627,12 +697,18 @@
         pltpu.VMEM((rows, qcols), bf16),
         pltpu.VMEM((requests, DRAFT, DRAFT), jnp.float32),
         pltpu.VMEM((requests, 1, DRAFT), jnp.float32),
-        pltpu.VMEM((2, rows, half // 2), bf16),
-        pltpu.VMEM((2, rows, half // 2), bf16),
-        pltpu.SemaphoreType.DMA((6,)),
-        pltpu.SemaphoreType.DMA((6,)),
+        pltpu.VMEM((rows, half * heads), bf16),
+        pltpu.VMEM((rows, qcols + HD), jnp.float32),
+        pltpu.VMEM((levels, rows, half // levels), bf16),
+        pltpu.VMEM((levels, rows, half // levels), bf16),
+        pltpu.VMEM((levels, rows, half // levels), bf16),
+        pltpu.SemaphoreType.DMA((3 + slots,)),
+        pltpu.SemaphoreType.DMA((3 + slots,)),
+        pltpu.SemaphoreType.DMA((levels,)),
+        pltpu.SemaphoreType.DMA((levels,)),
+        pltpu.SemaphoreType.DMA((2 * slots + 3,)),
     ]
-    for piece in range(4):
+    for piece in range(6):
         scratch += [pltpu.SemaphoreType.DMA((positions,))] * 4
         scratch += [pltpu.SemaphoreType.DMA((tok_count,))]
     return pl.pallas_call(
@@ -641,7 +717,7 @@
             jax.ShapeDtypeStruct(tokens.shape, bf16),
             jax.ShapeDtypeStruct(cache.shape, bf16),
         ),
-        in_specs=[vmem] * 6 + [smem] * 3,
+        in_specs=[hbm] * 5 + [vmem] + [smem] * 3,
         out_specs=(vmem, vmem),
         scratch_shapes=scratch,
         compiler_params=pltpu.CompilerParams(
@@ -671,8 +747,8 @@
         and tok_count >= 3 * XS * CORES
         and query_weight.shape[0] % TILE == 0
         and output_weight.shape[1] % TILE == 0
-        and output_weight.shape[1] > TILE
-        and (tokens.shape[1] // 2) % 128 == 0
+        and output_weight.shape[1] >= 3 * TILE
+        and XS * CORES * query_weight.shape[0] % 128 == 0
         and cache.shape[0] == NPR
         and parents.shape[0] == head_count
     )

time: 104 us -> 98.5 us (0.947)
  Pallas kernels: 93.7 us -> 88.9 us
    pallas_call x1, Pallas kernels: 93.7 us -> 88.9 us  [fused(): pl.pallas_call(fused_kernel, out_shape=(jax.ShapeDtypeStruct(tokens.shape...]
where the time goes in v2:
time: 98.5 us; the launch traced here: 98.2 us
  Pallas kernels  88.9 us (90%)
  local copies, waits for them, and re-layouts  8.61 us (9%)
    pallas_call x1, Pallas kernels, fused(): pl.pallas_call(fused_kernel, out_shape=(jax.ShapeDtypeStruct(tokens.shape...  88.9 us
    unnamed x20, local copies, waits for them, and re-layouts  8.61 us

profile of v2, /device:TPU:0, one launch (start us, length us, event | category | flops | bytes accessed | tf_op | source)
XLA Modules:
  0.0 98.2 jit_solution(11397926244601245032)
XLA Ops:
  0.6 0.0 copy-start.7
  0.6 0.0 copy-start.5
  0.7 0.6 copy-done.7
  1.3 0.0 copy-done.5
  1.3 0.0 copy-start
  1.3 1.1 %copy-done = bf16[160,2560]{1,0:T(8,128)(2,1)S(1)} copy-done((bf16[160,2560]{1,0:T(8,128)(2,1)S(1)}, bf16[160,2560]{1,0:T(8,128)(2,1)}, u32[]{:S(2)}) %copy-start) | copy-done | bytes 819224
  2.5 0.0 copy-start.1
  2.5 1.0 %copy-done.1 = bf16[4,2,128,256]{3,2,1,0:T(8,128)(2,1)S(1)} copy-done((bf16[4,2,128,256]{3,2,1,0:T(8,128)(2,1)S(1)}, bf16[4,2,128,256]{3,2,1,0:T(8,128)(2,1)}, u32[]{:S(2)}) %copy-start.1) | copy-done | bytes 524312
  3.5 0.0 copy-start.2
  3.5 1.0 %copy-done.2 = bf16[2560,80]{0,1:T(8,128)(2,1)S(1)} copy-done((bf16[2560,80]{0,1:T(8,128)(2,1)S(1)}, bf16[2560,80]{0,1:T(8,128)(2,1)}, u32[]{:S(2)}) %copy-start.2) | copy-done | bytes 409624
  4.5 0.0 copy-start.3
  4.5 1.0 copy-done.3
  5.5 0.0 copy-start.4
  5.5 0.9 copy-done.4
  6.4 0.0 copy-start.6
  6.4 0.7 copy-done.6
  7.1 0.0 copy-start.8
  7.1 0.7 copy-done.8
  7.7 88.9 %shard_map.104 = (bf16[128,1280]{1,0:T(8,128)(2,1)S(1)}, bf16[4,2,128,256]{3,2,1,0:T(8,128)(2,1)S(1)}) custom-call(bf16[128,1280]{1,0:T(8,128)(2,1)S(1)} %copy-done.3, bf16[160,2560]{1,0:T(8,128)(2,1)S(1)} %copy-done, bf16[160,512]{1,0:T(8,128)(2,1)S(1)} %copy-done.4, bf16[80,2560]{1,0:T(8,128)(2,1)S(1)} %bitcast.1, bf16[4,2,128,256]{3,2,1,0:T(8,128)(2,1)S(1)} %copy-done.1, ...), custom_call_target="tpu_custom_call" | custom-call | flops 1677721600 | bytes 4194304 | tf_op jit(solution)/shard_map/pallas_call | solution.py:714
  96.6 0.7 copy.13
  97.4 0.8 copy.14
Async XLA Ops:
  0.6 0.7 copy-start.7
  0.6 0.7 copy-start.5
  1.3 1.1 %copy-start = (bf16[160,2560]{1,0:T(8,128)(2,1)S(1)}, bf16[160,2560]{1,0:T(8,128)(2,1)}, u32[]{:S(2)}) copy-start(bf16[160,2560]{1,0:T(8,128)(2,1)} %qw_ref.1) | copy-start | bytes 2457604
  2.5 1.0 %copy-start.1 = (bf16[4,2,128,256]{3,2,1,0:T(8,128)(2,1)S(1)}, bf16[4,2,128,256]{3,2,1,0:T(8,128)(2,1)}, u32[]{:S(2)}) copy-start(bf16[4,2,128,256]{3,2,1,0:T(8,128)(2,1)} %cache_ref.1) | copy-start | bytes 1572868
  3.5 1.0 %copy-start.2 = (bf16[2560,80]{0,1:T(8,128)(2,1)S(1)}, bf16[2560,80]{0,1:T(8,128)(2,1)}, u32[]{:S(2)}) copy-start(bf16[2560,80]{0,1:T(8,128)(2,1)} %param.12) | copy-start | bytes 1228804
  4.5 1.0 copy-start.3
  5.5 0.9 copy-start.4
  6.4 0.7 copy-start.6
  7.1 0.7 copy-start.8

commit v3 on v2

--- a/solution.py
+++ b/solution.py
@@ -257,10 +257,16 @@
     psend,
     pown,
     precv,
+    fsend,
+    final,
     y_send,
     y_recv,
     part_send,
     part_recv,
+    final_send,
+    final_recv,
+    mix_send,
+    mix_recv,
     load_sem,
     *piece_sems,
 ):
@@ -269,7 +275,6 @@
     slots = qbuf.shape[0]
     rows = tok_ref.shape[0]
     narrow = wo_ref.shape[0]
-    main_rows = narrow - TILE
     requests = parents_ref.shape[0]
     level = XS * CORES
     part_rows = wbuf.shape[1]
@@ -343,109 +348,6 @@
             device_id_type=MESH,
         )
 
-    class Piece:
-        def __init__(self, view, sems, x_first):
-            self.view = view
-            self.up, self.down, self.xs, self.cs, self.recv = sems
-            self.x_first = x_first
-
-        def copy(self, t, sems, device):
-            ref = self.view(t)
-            return remote(ref, ref, sems.at[lax.div(t, CORES)], self.recv.at[t], device)
-
-        def along(self, t, act, up, down):
-            if up:
-                pl.when(has_up)(lambda: act(self.copy(t, self.up, up_dev)))
-            if down:
-                pl.when(has_down)(lambda: act(self.copy(t, self.down, down_dev)))
-
-        def spread(self, t, distance, own_x, act):
-            if own_x and (not self.x_first or distance == 0):
-                act(self.copy(t, self.xs, x_dev))
-            act(self.copy(t, self.cs, core_dev))
-
-        def arrive(self, t):
-            self.copy(t, self.cs, core_dev).wait_recv()
-
-        def visit(self, distance, sending, act, orders=(0, 1)):
-            xs = (xpos, 1 - xpos) if self.x_first else (xpos,)
-            for order, xx in enumerate(xs):
-                if order not in orders:
-                    continue
-                if distance == 0:
-                    t = tok_at(z, xx, core)
-                    if sending and order == 1:
-                        self.arrive(t)
-                    self.along(t, act, True, True)
-                    self.spread(t, 0, order == 0, act)
-                    continue
-
-                @pl.when(z - distance >= 0)
-                def _():
-                    t = tok_at(z - distance, xx, core)
-                    if sending:
-                        self.arrive(t)
-                    self.along(t, act, True, False)
-                    self.spread(t, distance, order == 0, act)
-
-                @pl.when(z + distance < levels)
-                def _():
-                    t = tok_at(z + distance, xx, core)
-                    if sending:
-                        self.arrive(t)
-                    self.along(t, act, False, True)
-                    self.spread(t, distance, order == 0, act)
-
-        def cross(self, distance, sending, act):
-            if self.x_first:
-                return
-            targets = [z] if distance == 0 else [z - distance, z + distance]
-            for index, zz in enumerate(targets):
-
-                def go(zz=zz):
-                    t = tok_at(zz, 1 - xpos, core)
-                    if sending:
-                        self.arrive(t)
-                    self.spread(t, distance, False, act)
-
-                if distance == 0:
-                    go()
-                else:
-                    pl.when(zz >= 0 if index == 0 else zz < levels)(go)
-
-        def step(self, distance, orders=(0, 1)):
-            self.visit(distance, True, lambda copy: copy.start(), orders)
-
-        def relay(self, distance):
-            self.cross(distance, True, lambda copy: copy.start())
-
-        def gathered(self, zz):
-            for xx in range(XS):
-                self.arrive(tok_at(zz, xx, 1 - core))
-
-        def drain(self):
-            for distance in range(levels):
-                self.visit(distance, False, lambda copy: copy.wait_send())
-                self.cross(distance, False, lambda copy: copy.wait_send())
-
-    pieces = [piece_sems[5 * i : 5 * i + 5] for i in range(6)]
-    cut = slots // 2 * HD
-    mid = main_rows // 2 // TILE * TILE
-    k_piece = Piece(lambda t: wbuf.at[t, :, qcols:], pieces[0], True)
-    qa_piece = Piece(lambda t: wbuf.at[t, :, :cut], pieces[1], False)
-    qb_piece = Piece(lambda t: wbuf.at[t, :, cut:qcols], pieces[2], False)
-    oa_piece = Piece(lambda t: obuf.at[:, t, :mid], pieces[3], False)
-    ob_piece = Piece(lambda t: obuf.at[:, t, mid:main_rows], pieces[4], False)
-    s_piece = Piece(lambda t: obuf.at[:, t, main_rows:], pieces[5], True)
-
-    def step(group, distance):
-        for piece in group:
-            piece.step(distance)
-
-    def relay(group, distance):
-        for piece in group:
-            piece.relay(distance)
-
     def each_level(distance, run):
         if distance == 0:
             run(z)
@@ -453,8 +355,91 @@
         pl.when(z - distance >= 0)(lambda: run(z - distance))
         pl.when(z + distance < levels)(lambda: run(z + distance))
 
-    weights = (k_piece, qa_piece, qb_piece)
-    outputs = (oa_piece, ob_piece, s_piece)
+    class Piece:
+        def __init__(self, view, sems, cross_x):
+            self.view = view
+            self.up, self.down, self.xs, self.cs, self.recv = sems
+            self.cross_x = cross_x
+
+        def copy(self, t, sems, device):
+            ref = self.view(t)
+            return remote(ref, ref, sems.at[lax.div(t, CORES)], self.recv.at[t], device)
+
+        def along(self, t, act, up, down):
+            if up:
+                pl.when(has_up)(lambda: act(self.copy(t, self.up, up_dev)))
+            if down:
+                pl.when(has_down)(lambda: act(self.copy(t, self.down, down_dev)))
+
+        def spread(self, t, own_x, act):
+            if own_x and self.cross_x:
+                act(self.copy(t, self.xs, x_dev))
+            act(self.copy(t, self.cs, core_dev))
+
+        def arrive(self, t):
+            self.copy(t, self.cs, core_dev).wait_recv()
+
+        def visit(self, distance, sending, act):
+            def go(zz, up, down):
+                t = tok_at(zz, xpos, core)
+                if sending and distance:
+                    self.arrive(t)
+                self.along(t, act, up, down)
+                self.spread(t, True, act)
+
+            if distance == 0:
+                go(z, True, True)
+                return
+            pl.when(z - distance >= 0)(lambda: go(z - distance, True, False))
+            pl.when(z + distance < levels)(lambda: go(z + distance, False, True))
+
+        def cross(self, distance, sending, act):
+            if not self.cross_x:
+                return
+
+            def go(zz):
+                t = tok_at(zz, 1 - xpos, core)
+                if sending:
+                    self.arrive(t)
+                self.spread(t, False, act)
+
+            each_level(distance, go)
+
+        def step(self, distance):
+            self.visit(distance, True, lambda copy: copy.start())
+
+        def relay(self, distance):
+            self.cross(distance, True, lambda copy: copy.start())
+
+        def gathered(self, zz):
+            self.arrive(tok_at(zz, xpos, 1 - core))
+            if self.cross_x:
+                self.arrive(tok_at(zz, 1 - xpos, 1 - core))
+
+        def drain(self):
+            for distance in range(levels):
+                self.visit(distance, False, lambda copy: copy.wait_send())
+                self.cross(distance, False, lambda copy: copy.wait_send())
+
+    pieces = [piece_sems[5 * i : 5 * i + 5] for i in range(4)]
+    cut = (slots + 1) // 2 * HD
+    mid = (narrow // 2 + TILE - 1) // TILE * TILE
+    weights = (
+        Piece(lambda t: wbuf.at[t, :, :cut], pieces[0], True),
+        Piece(lambda t: wbuf.at[t, :, cut:], pieces[1], True),
+    )
+    outputs = (
+        Piece(lambda t: obuf.at[:, t, :mid], pieces[2], False),
+        Piece(lambda t: obuf.at[:, t, mid:], pieces[3], False),
+    )
+
+    def step(group, distance):
+        for piece in group:
+            piece.step(distance)
+
+    def relay(group, distance):
+        for piece in group:
+            piece.relay(distance)
 
     wosends = [
         remote(
@@ -472,16 +457,10 @@
         copy.start()
     for load in loads[:weight_loads]:
         load.wait()
-    k_piece.step(0, (0,))
-    qa_piece.step(0)
-    qb_piece.step(0)
+    step(weights, 0)
     csend.start()
     for load in loads[weight_loads:]:
         load.wait()
-    k_piece.step(0, (1,))
-    for copy in wosends:
-        copy.wait_recv()
-    s_piece.step(0, (0,))
 
     row_ids = lax.broadcasted_iota(jnp.int32, (DRAFT, DRAFT), 0)
     col_ids = lax.broadcasted_iota(jnp.int32, (DRAFT, DRAFT), 1)
@@ -543,12 +522,12 @@
 
     step(weights, 1)
     relay(weights, 0)
-    s_piece.step(0, (1,))
     project(0)
     step(weights, 2)
     relay(weights, 1)
-    oa_piece.step(0)
-    ob_piece.step(0)
+    for copy in wosends:
+        copy.wait_recv()
+    step(outputs, 0)
     project(1)
     for distance in range(3, levels):
         step(weights, distance)
@@ -556,7 +535,6 @@
         if distance == 3:
             step(outputs, 1)
         project(distance - 1)
-    relay(outputs, 0)
     relay(weights, levels - 1)
     project(levels - 1)
 
@@ -573,7 +551,6 @@
     kvsend = remote(kvbuf.at[y], kvbuf.at[y], y_send.at[2], y_recv.at[2], y_dev)
     kvsend.start()
     step(outputs, 2)
-    relay(outputs, 1)
     for slot in range(slots):
         value = rotated(accum[:, slot * HD : (slot + 1) * HD])
         qbuf[slot] = (value * HD ** (-0.5)).astype(jnp.bfloat16)
@@ -608,7 +585,7 @@
         result = result + jnp.dot(tree, kvbuf[1, span, :], preferred_element_type=jnp.float32)
         result = result.astype(jnp.bfloat16)
         for slot in range(slots):
-            mixbuf[span, slot * HD : (slot + 1) * HD] = result[slot * DRAFT : (slot + 1) * DRAFT]
+            mixbuf[xpos, span, slot * HD : (slot + 1) * HD] = result[slot * DRAFT : (slot + 1) * DRAFT]
 
     def refresh_one():
         length = len_ref[y]
@@ -632,43 +609,69 @@
                 old = cbuf[y, page, entry].astype(jnp.float32)
                 cache_out_ref[page, entry] = jnp.where(written, placed, old).astype(jnp.bfloat16)
 
-    width = level * narrow
+    width = CORES * narrow
 
     def part_copy(zz):
         return remote(psend.at[zz], precv.at[zz], part_send.at[zz], part_recv.at[zz], y_dev)
+
+    def final_copy(zz):
+        ref = final.at[xpos, zz]
+        return remote(fsend.at[zz], ref, final_send.at[zz], final_recv.at[zz], x_dev)
+
+    def mix_copy(r):
+        ref = mixbuf.at[xpos, r * DRAFT : (r + 1) * DRAFT]
+        return remote(ref, ref, mix_send.at[r], mix_recv.at[r], x_dev)
 
     def output_level(zz):
         for piece in outputs:
             piece.gathered(zz)
-        mixed = mixbuf[...]
-        block = obuf[other, pl.ds(zz * level, level)].reshape(width, qcols)
+        mixed = mixbuf[...].reshape(XS * rows, qcols)
+        own = pl.ds(zz * level + xpos * CORES, CORES)
+        block = obuf[other, own].reshape(width, qcols)
         value = lax.dot_general(mixed, block, NT, preferred_element_type=jnp.float32)
-        psend[zz] = value.astype(jnp.bfloat16)
+        psend[zz] = value.astype(jnp.bfloat16).reshape(XS, rows, width)
         part_copy(zz).start()
-        block = obuf[y, pl.ds(zz * level, level)].reshape(width, qcols)
+        block = obuf[y, own].reshape(width, qcols)
         value = lax.dot_general(mixed, block, NT, preferred_element_type=jnp.float32)
-        pown[zz] = value.astype(jnp.bfloat16)
+        pown[zz] = value.astype(jnp.bfloat16).reshape(XS, rows, width)
+
+    def sum_level(zz):
+        part_copy(zz).wait_recv()
+
+        def summed(xx):
+            total = pown[zz, xx].astype(jnp.float32) + precv[zz, xx].astype(jnp.float32)
+            return total.astype(jnp.bfloat16)
+
+        fsend[zz] = summed(1 - xpos)
+        final_copy(zz).start()
+        final[xpos, zz] = summed(xpos)
 
     attend_one(0)
+    mix_copy(0).start()
     for distance in range(3, levels):
         step(outputs, distance)
-        relay(outputs, distance - 1)
     for r in range(1, requests):
         attend_one(r)
-    for distance in range(levels - 1):
+        mix_copy(r).start()
+    refresh_one()
+    for r in range(requests):
+        mix_copy(r).wait_recv()
+    for distance in range(levels):
         each_level(distance, output_level)
-    refresh_one()
-    relay(outputs, levels - 1)
-    each_level(levels - 1, output_level)
-    sums = []
+        if distance > 0:
+            each_level(distance - 1, sum_level)
+    each_level(levels - 1, sum_level)
     for zz in range(levels):
-        part_copy(zz).wait_recv()
-        sums.append(pown[zz].astype(jnp.float32) + precv[zz].astype(jnp.float32))
-    out_ref[...] = jnp.concatenate(sums, axis=1).astype(jnp.bfloat16)
+        final_copy(zz).wait_recv()
+    done = [final[xx, zz] for zz in range(levels) for xx in range(XS)]
+    out_ref[...] = jnp.concatenate(done, axis=1)
     for piece in weights + outputs:
         piece.drain()
-    for copy in [xsend, csend, kvsend] + wosends + [part_copy(zz) for zz in range(levels)]:
+    for copy in [xsend, csend, kvsend] + wosends + [mix_copy(r) for r in range(requests)]:
         copy.wait_send()
+    for zz in range(levels):
+        part_copy(zz).wait_send()
+        final_copy(zz).wait_send()
 
 
 def fused(tokens, query_weight, keyvalue_weight, output_weight, cache, page_table, parents, cache_len, accepted_leaf):
@@ -683,7 +686,7 @@
     qcols = slots * HD
     positions = tok_count // CORES
     levels = positions // XS
-    hbm = pl.BlockSpec(memory_space=pl.ANY)
+    hbm = pl.BlockSpec(memory_space=pltpu.HBM)
     vmem = pl.BlockSpec(memory_space=pltpu.VMEM)
     smem = pl.BlockSpec(memory_space=pltpu.SMEM)
     bf16 = jnp.bfloat16
@@ -694,21 +697,27 @@
         pltpu.VMEM((heads,) + cache.shape, bf16),
         pltpu.VMEM((2, rows, HD), bf16),
         pltpu.VMEM((slots, rows, HD), bf16),
-        pltpu.VMEM((rows, qcols), bf16),
+        pltpu.VMEM((XS, rows, qcols), bf16),
         pltpu.VMEM((requests, DRAFT, DRAFT), jnp.float32),
         pltpu.VMEM((requests, 1, DRAFT), jnp.float32),
         pltpu.VMEM((rows, half * heads), bf16),
         pltpu.VMEM((rows, qcols + HD), jnp.float32),
-        pltpu.VMEM((levels, rows, half // levels), bf16),
-        pltpu.VMEM((levels, rows, half // levels), bf16),
-        pltpu.VMEM((levels, rows, half // levels), bf16),
+        pltpu.VMEM((levels, XS, rows, CORES * narrow), bf16),
+        pltpu.VMEM((levels, XS, rows, CORES * narrow), bf16),
+        pltpu.VMEM((levels, XS, rows, CORES * narrow), bf16),
+        pltpu.VMEM((levels, rows, CORES * narrow), bf16),
+        pltpu.VMEM((XS, levels, rows, CORES * narrow), bf16),
         pltpu.SemaphoreType.DMA((3 + slots,)),
         pltpu.SemaphoreType.DMA((3 + slots,)),
         pltpu.SemaphoreType.DMA((levels,)),
         pltpu.SemaphoreType.DMA((levels,)),
+        pltpu.SemaphoreType.DMA((levels,)),
+        pltpu.SemaphoreType.DMA((levels,)),
+        pltpu.SemaphoreType.DMA((requests,)),
+        pltpu.SemaphoreType.DMA((requests,)),
         pltpu.SemaphoreType.DMA((2 * slots + 3,)),
     ]
-    for piece in range(6):
+    for piece in range(4):
         scratch += [pltpu.SemaphoreType.DMA((positions,))] * 4
         scratch += [pltpu.SemaphoreType.DMA((tok_count,))]
     return pl.pallas_call(
@@ -721,7 +730,7 @@
         out_specs=(vmem, vmem),
         scratch_shapes=scratch,
         compiler_params=pltpu.CompilerParams(
-            collective_id=0, has_side_effects=True, vmem_limit_bytes=48 * 1024 * 1024
+            collective_id=0, has_side_effects=True, vmem_limit_bytes=64 * 1024 * 1024
         ),
         cost_estimate=pl.CostEstimate(
             flops=4 * rows * HD * HQ * HD * 5, bytes_accessed=1 << 22, transcendentals=1 << 19

time: 98.5 us -> 95.4 us (0.969)
  local copies, waits for them, and re-layouts: 8.61 us -> 2.57 us
  Pallas kernels: 88.9 us -> 92 us
    unnamed x20 -> x4, local copies, waits for them, and re-layouts: 8.61 us -> 2.57 us
    pallas_call x1, Pallas kernels: 88.9 us -> 92 us  [fused(): pl.pallas_call(fused_kernel, out_shape=(jax.ShapeDtypeStruct(tokens.shape...]
where the time goes in v3:
time: 95.4 us; the launch traced here: 95.3 us
  Pallas kernels  92 us (96%)
  local copies, waits for them, and re-layouts  2.57 us (3%)
    pallas_call x1, Pallas kernels, fused(): pl.pallas_call(fused_kernel, out_shape=(jax.ShapeDtypeStruct(tokens.shape...  92 us
    unnamed x4, local copies, waits for them, and re-layouts  2.57 us

profile of v3, /device:TPU:0, one launch (start us, length us, event | category | flops | bytes accessed | tf_op | source)
XLA Modules:
  0.0 95.3 jit_solution(904190700002482678)
XLA Ops:
  0.6 92.0 %shard_map.104 = (bf16[128,1280]{1,0:T(8,128)(2,1)}, bf16[4,2,128,256]{3,2,1,0:T(8,128)(2,1)}) custom-call(bf16[128,1280]{1,0:T(8,128)(2,1)} %tok_ref.1, bf16[160,2560]{1,0:T(8,128)(2,1)} %qw_ref.1, bf16[160,512]{1,0:T(8,128)(2,1)} %kvw_ref.1, bf16[80,2560]{1,0:T(8,128)(2,1)} %bitcast.1, bf16[4,2,128,256]{3,2,1,0:T(8,128)(2,1)} %cache_ref.1, ...), custom_call_target="tpu_custom_call" | custom-call | flops 1677721600 | bytes 4194304 | tf_op jit(solution)/shard_map/pallas_call | solution.py:723
  92.7 0.0 copy-start
  92.7 1.8 %copy.13 = bf16[128,1280]{1,0:T(8,128)(2,1)} copy(bf16[128,1280]{1,0:T(8,128)(2,1)} %get-tuple-element.4) | data formatting | bytes 655360
  94.5 0.0 copy-done
  94.5 0.8 copy.14
Async XLA Ops:
  92.7 1.8 %copy-start = (bf16[4,2,128,256]{3,2,1,0:T(8,128)(2,1)S(1)}, bf16[4,2,128,256]{3,2,1,0:T(8,128)(2,1)}, u32[]{:S(2)}) copy-start(bf16[4,2,128,256]{3,2,1,0:T(8,128)(2,1)} %get-tuple-element.5) | copy-start | bytes 1572868

commit v4 on v3

--- a/solution.py
+++ b/solution.py
@@ -421,12 +421,13 @@
                 self.visit(distance, False, lambda copy: copy.wait_send())
                 self.cross(distance, False, lambda copy: copy.wait_send())
 
-    pieces = [piece_sems[5 * i : 5 * i + 5] for i in range(4)]
-    cut = (slots + 1) // 2 * HD
+    pieces = [piece_sems[5 * i : 5 * i + 5] for i in range(5)]
+    cut = (slots + 1) // 3 * HD
     mid = (narrow // 2 + TILE - 1) // TILE * TILE
     weights = (
         Piece(lambda t: wbuf.at[t, :, :cut], pieces[0], True),
-        Piece(lambda t: wbuf.at[t, :, cut:], pieces[1], True),
+        Piece(lambda t: wbuf.at[t, :, cut : 2 * cut], pieces[1], True),
+        Piece(lambda t: wbuf.at[t, :, 2 * cut :], pieces[4], True),
     )
     outputs = (
         Piece(lambda t: obuf.at[:, t, :mid], pieces[2], False),
@@ -653,13 +654,13 @@
     for r in range(1, requests):
         attend_one(r)
         mix_copy(r).start()
-    refresh_one()
     for r in range(requests):
         mix_copy(r).wait_recv()
     for distance in range(levels):
         each_level(distance, output_level)
         if distance > 0:
             each_level(distance - 1, sum_level)
+    refresh_one()
     each_level(levels - 1, sum_level)
     for zz in range(levels):
         final_copy(zz).wait_recv()
@@ -717,7 +718,7 @@
         pltpu.SemaphoreType.DMA((requests,)),
         pltpu.SemaphoreType.DMA((2 * slots + 3,)),
     ]
-    for piece in range(4):
+    for piece in range(5):
         scratch += [pltpu.SemaphoreType.DMA((positions,))] * 4
         scratch += [pltpu.SemaphoreType.DMA((tok_count,))]
     return pl.pallas_call(

time: 95.4 us -> 96 us (level)
  no operation moved by 1% of the time
where the time goes in v4:
time: 96 us; the launch traced here: 95.8 us
  Pallas kernels  92.6 us (96%)
  local copies, waits for them, and re-layouts  2.57 us (3%)
    pallas_call x1, Pallas kernels, fused(): pl.pallas_call(fused_kernel, out_shape=(jax.ShapeDtypeStruct(tokens.shape...  92.6 us
    unnamed x4, local copies, waits for them, and re-layouts  2.57 us

profile of v4, /device:TPU:0, one launch (start us, length us, event | category | flops | bytes accessed | tf_op | source)
XLA Modules:
  0.0 95.8 jit_solution(3226027117262304199)
XLA Ops:
  0.6 92.6 %shard_map.104 = (bf16[128,1280]{1,0:T(8,128)(2,1)}, bf16[4,2,128,256]{3,2,1,0:T(8,128)(2,1)}) custom-call(bf16[128,1280]{1,0:T(8,128)(2,1)} %tok_ref.1, bf16[160,2560]{1,0:T(8,128)(2,1)} %qw_ref.1, bf16[160,512]{1,0:T(8,128)(2,1)} %kvw_ref.1, bf16[80,2560]{1,0:T(8,128)(2,1)} %bitcast.1, bf16[4,2,128,256]{3,2,1,0:T(8,128)(2,1)} %cache_ref.1, ...), custom_call_target="tpu_custom_call" | custom-call | flops 1677721600 | bytes 4194304 | tf_op jit(solution)/shard_map/pallas_call | solution.py:724
  93.2 0.0 copy-start
  93.2 1.8 %copy.13 = bf16[128,1280]{1,0:T(8,128)(2,1)} copy(bf16[128,1280]{1,0:T(8,128)(2,1)} %get-tuple-element.4) | data formatting | bytes 655360
  95.0 0.0 copy-done
  95.0 0.8 copy.14
Async XLA Ops:
  93.2 1.8 %copy-start = (bf16[4,2,128,256]{3,2,1,0:T(8,128)(2,1)S(1)}, bf16[4,2,128,256]{3,2,1,0:T(8,128)(2,1)}, u32[]{:S(2)}) copy-start(bf16[4,2,128,256]{3,2,1,0:T(8,128)(2,1)} %get-tuple-element.5) | copy-start | bytes 1572868
